TPU v7x, 32 devices: a whole 2x2x4 slice. The times are simulated.
32 devices in a mesh: row: 4 (over y, x), col: 8 (over z, core).
Axes of the slice: x: 2, y: 2, z: 4, core: 2. Of those that a mesh axis runs over, the one named last changes fastest.
Arguments:
- anomalies: bfloat16 [128, 256, 1024], P('row', 'col'), may hold values from -6 to 6
- kappa: bfloat16 [128, 256], P('row', 'col'), may hold values from 0.039794922 to 0.23925781
- members: int32 [1024], replicated, may hold values from 0 to 7
- months: int32 [1024], replicated, may hold values from 0 to 11
- land: int32 [128, 256], P('row', 'col'), may hold values 0 or 1
Outputs:
- covariance: bfloat16 [32768, 32768], P('row', 'col')
All inputs are finite; a program needn't handle non-finite values. No bound on the sum of `land` on one device may be relied on, other than what follows from the above.
Results may differ from a plain program's by a relative error of at most 0.0053.
Values may be sent and summed in bfloat16 or wider, within the bound.
A program may use at most 192 MiB of HBM per device.

v0:
```python
import math

import jax
import jax.numpy as jnp
from jax import lax
from jax.sharding import PartitionSpec as P

LAT = 128
MAPS = 1024
MONTHS = 12
STEPS = 4
TILE = 2048
GROUPS = 96


def extended(array, sides, width, wrap):
    for axis, dim in sides:
        size, length = (lax.axis_size(axis), array.shape[dim])
        up = [(i, (i + 1) % size) for i in range(size if wrap else size - 1)]
        down = [(j, i) for i, j in up]
        last = lax.slice_in_dim(array, length - width, length, axis=dim)
        first = lax.slice_in_dim(array, 0, width, axis=dim)
        before = lax.ppermute(last, axis, up)
        after = lax.ppermute(first, axis, down)
        array = jnp.concatenate([before, array, after], axis=dim)
    return array


def from_root(array, axis, root):
    mine = lax.axis_index(axis) == root
    return lax.psum(jnp.where(mine, array, jnp.zeros_like(array)), axis)


def centre_maps(field, weights, onehot, counts):
    lat_rows, lon_cols, maps = field.shape
    flat = field.reshape(lat_rows * lon_cols, maps)
    sums = jnp.dot(flat, onehot, precision=lax.Precision.HIGHEST)
    back = jnp.dot(sums / counts, onehot.T, precision=lax.Precision.HIGHEST)
    centred = ((flat - back) * weights.reshape(lat_rows * lon_cols, 1)).astype(jnp.bfloat16)
    return centred.reshape(lat_rows, lon_cols, maps)


def per_device(anomalies, kappa, members, months, land):
    lat_rows = anomalies.shape[0]
    maps = anomalies.shape[2]
    row_index = lax.axis_index("row")
    col_index = lax.axis_index("col")
    lat_ids = row_index * lat_rows + jnp.arange(lat_rows, dtype=jnp.int32)
    phi = ((lat_ids.astype(jnp.float32) + 0.5) / LAT - 0.5) * math.pi
    lat_weight = jnp.sqrt(jnp.cos(phi))
    sea_weight = jnp.where(land == 1, 1.0, 0.5).astype(jnp.float32)
    cell_weight = sea_weight * lat_weight[:, None]
    groups = members * MONTHS + months
    onehot = (groups[:, None] == jnp.arange(GROUPS, dtype=jnp.int32)[None, :]).astype(jnp.float32)
    counts = jnp.maximum(jnp.sum(onehot, axis=0), 1.0)
    field = anomalies.astype(jnp.float32)
    coeff = kappa.astype(jnp.float32)[:, :, None]
    for step in range(STEPS):
        north_south = extended(field, (("row", 0),), 1, False)
        east_west = extended(field, (("col", 1),), 1, True)
        beside = north_south[2:] + north_south[:-2] + (east_west[:, 2:] + east_west[:, :-2])
        field = field + coeff * (beside - 4.0 * field)
    block = centre_maps(field, cell_weight, onehot, counts)
    band = lax.all_gather(block, "col", axis=1, tiled=True)
    ratio = lax.axis_size("col") // lax.axis_size("row")
    panel_lats = lat_rows // ratio
    half = lax.dynamic_slice_in_dim(band, col_index % ratio * panel_lats, panel_lats, 0)
    panel = from_root(half, "row", col_index // ratio)
    left = band.reshape(-1, maps)
    right = panel.reshape(-1, maps)
    rows_dev = left.shape[0]
    cols_dev = right.shape[0]
    col_tile = (col_index * cols_dev + jnp.arange(cols_dev, dtype=jnp.int32)) // TILE
    whole = (
        lax.dot_general(left, right, (((1,), (1,)), ((), ())), preferred_element_type=jnp.float32)
        / MAPS
    )
    row_tile = (row_index * rows_dev + jnp.arange(rows_dev, dtype=jnp.int32)) // TILE
    whole = jnp.where(col_tile[None, :] >= row_tile[:, None], whole, 0.0)
    return whole.astype(jnp.bfloat16)


def solution(mesh):
    placed = (P("row", "col", None), P("row", "col"), P(), P(), P("row", "col"))
    return jax.shard_map(
        per_device, mesh=mesh, in_specs=placed, out_specs=P("row", "col"), check_vma=False
    )
```

profile of v0, /device:TPU:1, one launch (start us, length us, event | category | flops | bytes accessed | tf_op | source)
XLA Modules:
  0.0 514.3 jit_solution(13107255597092466524)
XLA Ops:
  6.5 1.4 fusion.39
  8.0 2.7 collective-permute-start.3
  10.8 0.9 fusion.38
  11.7 1.3 collective-permute-start
  13.0 4.0 collective-permute-start.1
  17.0 4.1 convert_element_type.22
  21.5 10.7 %fusion.22 = f32[32,32,1024]{2,1,0:T(8,128)S(1)} fusion(f32[32,32,1024]{2,1,0:T(8,128)} %convert_element_type.22, f32[32,1,1024]{2,1,0:T(1,128)S(1)} %copy.28, f32[32,1,1024]{2,1,0:T(1,128)S(1)} %copy.26, f32[1,32,1024]{2,1,0:T(8,128)S(1)} %collective-permute-done.1, f32[1,32,1024]{2,1,0:T(8,128)S(1)} %collective-permute-done, ...), kind=kLoop, calls=%fused_computation.37 | loop fusion | flops 11534336 | bytes 8916992 | tf_op jit(solution)/shard_map/add | solution.py:62
  32.5 2.3 collective-permute-start.7
  35.0 1.3 collective-permute-start.4
  36.3 5.1 collective-permute-start.5
  41.9 1.5 collective-permute-done.5
  43.4 3.1 fusion.16
  46.7 1.8 copy-done
  48.6 2.3 collective-permute-start.11
  50.9 2.1 collective-permute-start.10
  53.0 1.3 collective-permute-start.8
  54.3 5.2 %collective-permute-start.9 = (f32[1,32,1024]{2,1,0:T(8,128)S(1)}, f32[1,32,1024]{2,1,0:T(8,128)S(1)}, u32[]{:S(2)}, u32[]{:S(2)}) collective-permute-start(f32[1,32,1024]{2,1,0:T(8,128)S(1)} %get-tuple-element.10), channel_id=1, source_target_pairs={{0,8},{8,16},{16,24},{1,9},{9,17},{17,25},{2,10},{10,18},{18,26},{... | collective-permute-start | bytes 393224 | tf_op jit(solution)/shard_map/ppermute | solution.py:23
  60.0 1.4 collective-permute-done.9
  61.4 10.6 %fusion.10 = f32[32,32,1024]{2,1,0:T(8,128)S(1)} fusion(f32[32,32,1024]{2,1,0:T(8,128)} %copy-done, f32[32,1,1024]{2,1,0:T(1,128)S(1)} %copy.36, f32[32,1,1024]{2,1,0:T(1,128)S(1)} %copy.34, f32[1,32,1024]{2,1,0:T(8,128)S(1)} %collective-permute-done.9, f32[1,32,1024]{2,1,0:T(8,128)S(1)} %collective-permute-done.8, f32[32,32]{1,0:T(8,128)S(1)} %convert_element_type.23), kind=kLoop, calls=%fused_computation.17 | loop fusion | flops 11534336 | bytes 8916992 | tf_op jit(solution)/shard_map/add | solution.py:62
  72.4 0.6 collective-permute-start.15
  73.0 3.9 collective-permute-start.14
  76.8 1.3 collective-permute-start.12
  78.1 5.8 %collective-permute-start.13 = (f32[1,32,1024]{2,1,0:T(8,128)S(1)}, f32[1,32,1024]{2,1,0:T(8,128)S(1)}, u32[]{:S(2)}, u32[]{:S(2)}) collective-permute-start(f32[1,32,1024]{2,1,0:T(8,128)S(1)} %get-tuple-element.6), channel_id=1, source_target_pairs={{0,8},{8,16},{16,24},{1,9},{9,17},{17,25},{2,10},{10,18},{18,26},{... | collective-permute-start | bytes 393224 | tf_op jit(solution)/shard_map/ppermute | solution.py:23
  84.3 1.4 collective-permute-done.13
  85.7 3.0 fusion.4
  88.7 2.3 convolution_divide_fusion
  91.0 3.5 multiply_convert_fusion
  94.6 0.3 all-reduce.2.cloned.1.call-start
  94.9 156.6 %all-gather.2.cloned.1.call-done = bf16[32,256,1024]{2,1,0:T(8,128)(2,1)} async-done(((bf16[32,32,1024]{2,1,0:T(8,128)(2,1)}), bf16[32,256,1024]{2,1,0:T(8,128)(2,1)}) %all-gather.2.cloned.1.call-update) | async-done | bytes 16777232 | tf_op jit(solution)/shard_map/all_gather | solution.py:64
  251.5 7.3 %dynamic-slice_select_fusion = bf16[16,256,1024]{2,1,0:T(8,128)(2,1)} fusion(bf16[32,256,1024]{2,1,0:T(8,128)(2,1)} %all-gather.2.cloned.1.call-done, s32[]{:T(128)S(6)} %select_n.54, pred[]{:T(512)S(6)} %eq.29), kind=kLoop, calls=%fused_computation.1 | loop fusion | flops 4194304 | bytes 16777220 | tf_op jit(solution)/shard_map/jit(_where)/select_n | solution.py:31
  258.9 169.9 %all-reduce.2.cloned.1.call-done = bf16[4096,1024]{1,0:T(8,128)(2,1)} async-done(((bf16[4096,1024]{1,0:T(8,128)(2,1)}), bf16[4096,1024]{1,0:T(8,128)(2,1)}) %all-reduce.2.cloned.1.call-update) | async-done | bytes 8388624 | tf_op jit(solution)/shard_map/psum | solution.py:31
  428.8 78.6 %select_convert_fusion = bf16[8192,4096]{1,0:T(8,128)(2,1)} fusion(bf16[8192,1024]{1,0:T(8,128)(2,1)} %bitcast.12, bf16[4096,1024]{1,0:T(8,128)(2,1)} %all-reduce.2.cloned.1.call-done, s32[4096]{0:T(1024)S(1)} %add_select_fusion.1, s32[8192]{0:T(1024)S(1)} %add_select_fusion), kind=kOutput, calls=%fused_computation | convolution fusion | flops 68853694464 | bytes 92323840 | tf_op jit(solution)/shard_map/dot_general | solution.py:75
  (58 shorter events, 2.8 us)
Async XLA Ops:
  6.5 14.6 %copy-start.2 = (bf16[32,32]{1,0:T(8,128)(2,1)S(1)}, bf16[32,32]{1,0:T(8,128)(2,1)}, u32[]{:S(2)}) copy-start(bf16[32,32]{1,0:T(8,128)(2,1)} %param.6) | copy-start | bytes 6148
  6.5 244.9 %all-gather.2.cloned.1.call-start = ((), (), s32[]{:S(2)}) async-start(), calls=%async_computation | async-start | bytes 18874368 | tf_op jit(solution)/shard_map/all_gather | solution.py:64
  8.0 13.2 %collective-permute-start.3 = (f32[32,1,1024]{2,0,1:T(8,128)S(1)}, f32[32,1,1024]{2,0,1:T(8,128)S(1)}, u32[]{:S(2)}, u32[]{:S(2)}) collective-permute-start(f32[32,1,1024]{2,0,1:T(8,128)S(1)} %copy.27), channel_id=1, source_target_pairs={{0,1},{1,2},{2,3},{3,4},{4,5},{5,6},{6,7},{7,0},{8,9},{9,10},{10,1... | collective-permute-start | bytes 393224 | tf_op jit(solution)/shard_map/ppermute | solution.py:23
  10.7 10.6 %collective-permute-start.2 = (f32[32,1,1024]{2,0,1:T(8,128)S(1)}, f32[32,1,1024]{2,0,1:T(8,128)S(1)}, u32[]{:S(2)}, u32[]{:S(2)}) collective-permute-start(f32[32,1,1024]{2,0,1:T(8,128)S(1)} %copy.25), channel_id=1, source_target_pairs={{1,0},{2,1},{3,2},{4,3},{5,4},{6,5},{7,6},{0,7},{9,8},{10,9},{11,1... | collective-permute-start | bytes 393224 | tf_op jit(solution)/shard_map/ppermute | solution.py:24
  11.7 9.8 %collective-permute-start = (f32[1,32,1024]{2,1,0:T(8,128)S(1)}, f32[1,32,1024]{2,1,0:T(8,128)S(1)}, u32[]{:S(2)}, u32[]{:S(2)}) collective-permute-start(f32[1,32,1024]{2,1,0:T(8,128)S(1)} %get-tuple-element.17), channel_id=1, source_target_pairs={{8,0},{16,8},{24,16},{9,1},{17,9},{25,17},{10,2},{18,10},{26,18},{... | collective-permute-start | bytes 393224 | tf_op jit(solution)/shard_map/ppermute | solution.py:24
  13.0 8.5 %collective-permute-start.1 = (f32[1,32,1024]{2,1,0:T(8,128)S(1)}, f32[1,32,1024]{2,1,0:T(8,128)S(1)}, u32[]{:S(2)}, u32[]{:S(2)}) collective-permute-start(f32[1,32,1024]{2,1,0:T(8,128)S(1)} %get-tuple-element.18), channel_id=1, source_target_pairs={{0,8},{8,16},{16,24},{1,9},{9,17},{17,25},{2,10},{10,18},{18,26},{... | collective-permute-start | bytes 393224 | tf_op jit(solution)/shard_map/ppermute | solution.py:23
  21.5 20.0 %copy-start.1 = (s32[32,32]{1,0:T(8,128)S(1)}, s32[32,32]{1,0:T(8,128)}, u32[]{:S(2)}) copy-start(s32[32,32]{1,0:T(8,128)} %param.9) | copy-start | bytes 12292
  32.5 9.1 %collective-permute-start.7 = (f32[32,1,1024]{2,0,1:T(8,128)S(1)}, f32[32,1,1024]{2,0,1:T(8,128)S(1)}, u32[]{:S(2)}, u32[]{:S(2)}) collective-permute-start(f32[32,1,1024]{2,0,1:T(8,128)S(1)} %copy.31), channel_id=1, source_target_pairs={{0,1},{1,2},{2,3},{3,4},{4,5},{5,6},{6,7},{7,0},{8,9},{9,10},{10,1... | collective-permute-start | bytes 393224 | tf_op jit(solution)/shard_map/ppermute | solution.py:23
  34.8 6.9 %collective-permute-start.6 = (f32[32,1,1024]{2,0,1:T(8,128)S(1)}, f32[32,1,1024]{2,0,1:T(8,128)S(1)}, u32[]{:S(2)}, u32[]{:S(2)}) collective-permute-start(f32[32,1,1024]{2,0,1:T(8,128)S(1)} %copy.29), channel_id=1, source_target_pairs={{1,0},{2,1},{3,2},{4,3},{5,4},{6,5},{7,6},{0,7},{9,8},{10,9},{11,1... | collective-permute-start | bytes 393224 | tf_op jit(solution)/shard_map/ppermute | solution.py:24
  35.0 6.8 %collective-permute-start.4 = (f32[1,32,1024]{2,1,0:T(8,128)S(1)}, f32[1,32,1024]{2,1,0:T(8,128)S(1)}, u32[]{:S(2)}, u32[]{:S(2)}) collective-permute-start(f32[1,32,1024]{2,1,0:T(8,128)S(1)} %get-tuple-element.13), channel_id=1, source_target_pairs={{8,0},{16,8},{24,16},{9,1},{17,9},{25,17},{10,2},{18,10},{26,18},{... | collective-permute-start | bytes 393224 | tf_op jit(solution)/shard_map/ppermute | solution.py:24
  36.3 7.1 %collective-permute-start.5 = (f32[1,32,1024]{2,1,0:T(8,128)S(1)}, f32[1,32,1024]{2,1,0:T(8,128)S(1)}, u32[]{:S(2)}, u32[]{:S(2)}) collective-permute-start(f32[1,32,1024]{2,1,0:T(8,128)S(1)} %get-tuple-element.14), channel_id=1, source_target_pairs={{0,8},{8,16},{16,24},{1,9},{9,17},{17,25},{2,10},{10,18},{18,26},{... | collective-permute-start | bytes 393224 | tf_op jit(solution)/shard_map/ppermute | solution.py:23
  41.8 17.7 %copy-start.3 = (s32[1024]{0:T(1024)S(1)}, s32[1024]{0:T(1024)}, u32[]{:S(2)}) copy-start(s32[1024]{0:T(1024)} %param.8) | copy-start | bytes 12292
  41.8 17.7 %copy-start.4 = (s32[1024]{0:T(1024)S(1)}, s32[1024]{0:T(1024)}, u32[]{:S(2)}) copy-start(s32[1024]{0:T(1024)} %param.7) | copy-start | bytes 12292
  46.5 2.0 copy-start
  48.6 11.2 %collective-permute-start.11 = (f32[32,1,1024]{2,0,1:T(8,128)S(1)}, f32[32,1,1024]{2,0,1:T(8,128)S(1)}, u32[]{:S(2)}, u32[]{:S(2)}) collective-permute-start(f32[32,1,1024]{2,0,1:T(8,128)S(1)} %copy.35), channel_id=1, source_target_pairs={{0,1},{1,2},{2,3},{3,4},{4,5},{5,6},{6,7},{7,0},{8,9},{9,10},{10,1... | collective-permute-start | bytes 393224 | tf_op jit(solution)/shard_map/ppermute | solution.py:23
  50.9 9.0 %collective-permute-start.10 = (f32[32,1,1024]{2,0,1:T(8,128)S(1)}, f32[32,1,1024]{2,0,1:T(8,128)S(1)}, u32[]{:S(2)}, u32[]{:S(2)}) collective-permute-start(f32[32,1,1024]{2,0,1:T(8,128)S(1)} %copy.33), channel_id=1, source_target_pairs={{1,0},{2,1},{3,2},{4,3},{5,4},{6,5},{7,6},{0,7},{9,8},{10,9},{11,1... | collective-permute-start | bytes 393224 | tf_op jit(solution)/shard_map/ppermute | solution.py:24
  53.0 7.0 %collective-permute-start.8 = (f32[1,32,1024]{2,1,0:T(8,128)S(1)}, f32[1,32,1024]{2,1,0:T(8,128)S(1)}, u32[]{:S(2)}, u32[]{:S(2)}) collective-permute-start(f32[1,32,1024]{2,1,0:T(8,128)S(1)} %get-tuple-element.9), channel_id=1, source_target_pairs={{8,0},{16,8},{24,16},{9,1},{17,9},{25,17},{10,2},{18,10},{26,18},{... | collective-permute-start | bytes 393224 | tf_op jit(solution)/shard_map/ppermute | solution.py:24
  54.3 7.1 %collective-permute-start.9 = (f32[1,32,1024]{2,1,0:T(8,128)S(1)}, f32[1,32,1024]{2,1,0:T(8,128)S(1)}, u32[]{:S(2)}, u32[]{:S(2)}) collective-permute-start(f32[1,32,1024]{2,1,0:T(8,128)S(1)} %get-tuple-element.10), channel_id=1, source_target_pairs={{0,8},{8,16},{16,24},{1,9},{9,17},{17,25},{2,10},{10,18},{18,26},{... | collective-permute-start | bytes 393224 | tf_op jit(solution)/shard_map/ppermute | solution.py:23
  72.4 11.5 %collective-permute-start.15 = (f32[32,1,1024]{2,0,1:T(8,128)S(1)}, f32[32,1,1024]{2,0,1:T(8,128)S(1)}, u32[]{:S(2)}, u32[]{:S(2)}) collective-permute-start(f32[32,1,1024]{2,0,1:T(8,128)S(1)} %copy.39), channel_id=1, source_target_pairs={{0,1},{1,2},{2,3},{3,4},{4,5},{5,6},{6,7},{7,0},{8,9},{9,10},{10,1... | collective-permute-start | bytes 393224 | tf_op jit(solution)/shard_map/ppermute | solution.py:23
  73.0 11.1 %collective-permute-start.14 = (f32[32,1,1024]{2,0,1:T(8,128)S(1)}, f32[32,1,1024]{2,0,1:T(8,128)S(1)}, u32[]{:S(2)}, u32[]{:S(2)}) collective-permute-start(f32[32,1,1024]{2,0,1:T(8,128)S(1)} %copy.37), channel_id=1, source_target_pairs={{1,0},{2,1},{3,2},{4,3},{5,4},{6,5},{7,6},{0,7},{9,8},{10,9},{11,1... | collective-permute-start | bytes 393224 | tf_op jit(solution)/shard_map/ppermute | solution.py:24
  76.8 7.4 %collective-permute-start.12 = (f32[1,32,1024]{2,1,0:T(8,128)S(1)}, f32[1,32,1024]{2,1,0:T(8,128)S(1)}, u32[]{:S(2)}, u32[]{:S(2)}) collective-permute-start(f32[1,32,1024]{2,1,0:T(8,128)S(1)} %get-tuple-element.5), channel_id=1, source_target_pairs={{8,0},{16,8},{24,16},{9,1},{17,9},{25,17},{10,2},{18,10},{26,18},{... | collective-permute-start | bytes 393224 | tf_op jit(solution)/shard_map/ppermute | solution.py:24
  78.1 7.5 %collective-permute-start.13 = (f32[1,32,1024]{2,1,0:T(8,128)S(1)}, f32[1,32,1024]{2,1,0:T(8,128)S(1)}, u32[]{:S(2)}, u32[]{:S(2)}) collective-permute-start(f32[1,32,1024]{2,1,0:T(8,128)S(1)} %get-tuple-element.6), channel_id=1, source_target_pairs={{0,8},{8,16},{16,24},{1,9},{9,17},{17,25},{2,10},{10,18},{18,26},{... | collective-permute-start | bytes 393224 | tf_op jit(solution)/shard_map/ppermute | solution.py:23
  94.6 334.2 %all-reduce.2.cloned.1.call-start = ((), (), s32[]{:S(2)}) async-start(), calls=%async_computation.1 | async-start | bytes 16777216 | tf_op jit(solution)/shard_map/psum | solution.py:31
Sparse Core Ops, SparseCore 0:
  94.7 156.7 all-gather.1
  258.9 169.8 all-reduce.1
where the time goes:
time: 515 us; the launch traced here: 514 us
  waiting for transfers between devices  331 us (64%)
  matrix products  84.5 us (16%)
  starting transfers between devices  39.7 us (8%)
  other arithmetic  39.1 us (8%)
  between operations  13.9 us (3%)
  local copies, waits for them, and re-layouts  6.17 us (1%)
    psum x1, waiting for transfers between devices, from_root(): return lax.psum(jnp.where(mine, array, jnp.zeros_like(array)), axis)  170 us
    all_gather x1, waiting for transfers between devices, per_device(): band = lax.all_gather(block, 'col', axis=1, tiled=True)  157 us
    dot_general x1, matrix products, per_device(): lax.dot_general(left, right, (((1,), (1,)), ((), ())), preferred_element_...  78.6 us
    ppermute x8, starting transfers between devices, extended(): before = lax.ppermute(last, axis, up)  28.1 us
    add x4, other arithmetic, per_device(): field = field + coeff * (beside - 4.0 * field)  27.4 us
    ppermute x8, starting transfers between devices, extended(): after = lax.ppermute(first, axis, down)  11.4 us
  transfers between devices with their start and end apart: 18, of which 5 were waited for; matrix products, arithmetic and copies ran while one was open for 1% of the time, Pallas kernels for 0%

commit v1 on v0

v1 whole, which is shorter than its diff:
```python
import functools
import math

import jax
import jax.numpy as jnp
from jax import lax
from jax.experimental import pallas as pl
from jax.experimental.pallas import tpu as pltpu
from jax.sharding import PartitionSpec as P

LAT = 128
MONTHS = 12
STEPS = 4
TILE = 2048
GROUPS = 96
MESH = pl.DeviceIdType.MESH
VMEM_LIMIT = 56 * 1024 * 1024


def extended(array, axis, dim, width, wrap):
    size, length = (lax.axis_size(axis), array.shape[dim])
    up = [(i, (i + 1) % size) for i in range(size if wrap else size - 1)]
    down = [(j, i) for i, j in up]
    last = lax.slice_in_dim(array, length - width, length, axis=dim)
    first = lax.slice_in_dim(array, 0, width, axis=dim)
    before = lax.ppermute(last, axis, up)
    after = lax.ppermute(first, axis, down)
    return jnp.concatenate([before, array, after], axis=dim)


def centre_maps(field, weights, onehot, counts):
    lat_rows, lon_cols, maps = field.shape
    flat = field.reshape(lat_rows * lon_cols, maps)
    sums = jnp.dot(flat, onehot, precision=lax.Precision.HIGHEST)
    back = jnp.dot(sums / counts, onehot.T, precision=lax.Precision.HIGHEST)
    centred = ((flat - back) * weights.reshape(lat_rows * lon_cols, 1)).astype(jnp.bfloat16)
    return centred.reshape(lat_rows, lon_cols, maps)


def ring_place(r, size):
    half = size // 2
    return jnp.where(r % 2 == 0, r // 2, size - 1 - r // 2), half


def ring_row(place, size):
    place = lax.rem(place + size, size)
    return jnp.where(place < size // 2, 2 * place, 2 * (size - 1 - place) + 1)


def gather_kernel(
    rows, chips, tile_lats, x, band, panel,
    local_sem, root_sem, chain_send, chain_recv, pair_send, pair_recv, ring_send, ring_recv,
):
    r = lax.axis_index("row")
    c = lax.axis_index("col")
    z = c // 2
    k = c % 2
    tiles = x.shape[0] // tile_lats
    mine = tiles // 2
    part = tile_lats // 2
    slots = tiles * chips
    lag = 2
    place, _ = ring_place(r, rows)
    root_place, _ = ring_place(z, rows)
    ring_to = (ring_row(place + 1, rows), ring_row(place - 1, rows))
    hops = (lax.rem(place - root_place + rows, rows), lax.rem(root_place - place + rows, rows))
    is_root = r == z
    has_next = (z < chips - 1, z > 0)
    step = (1, -1)

    def signal(row, col):
        pl.semaphore_signal(barrier, inc=1, device_id=(row, col), device_id_type=MESH)

    barrier = pltpu.get_barrier_semaphore()
    signal(r, 2 * z + 1 - k)
    signal(ring_to[0], c)
    signal(ring_to[1], c)
    for way in range(2):
        @pl.when(has_next[way])
        def _(way=way):
            signal(r, c + 2 * step[way])
    pl.semaphore_wait(
        barrier, 3 + has_next[0].astype(jnp.int32) + has_next[1].astype(jnp.int32))

    def slot_of(i):
        j = i // chips
        return (j % 2) * mine + j // 2, i % chips

    def lats(q):
        return pl.ds(q * tile_lats, tile_lats)

    def source_chip(way, t):
        return z - step[way] * t

    def valid(way, t):
        chip = source_chip(way, t)
        ok = jnp.logical_and(chip >= 0, chip < chips)
        return ok if way == 0 else jnp.logical_and(ok, t > 0)

    def local(q):
        return pltpu.make_async_copy(x.at[lats(q)], band.at[lats(q), c], local_sem.at[q])

    def chain(way, q, t, own):
        block = 2 * source_chip(way, t) + k
        return pltpu.make_async_remote_copy(
            src_ref=x.at[lats(q)] if own else band.at[lats(q), block],
            dst_ref=band.at[lats(q), block],
            send_sem=chain_send.at[way, q, t],
            recv_sem=chain_recv.at[way, q, t],
            device_id=(r, c + 2 * step[way]),
            device_id_type=MESH,
        )

    def pair(way, q, t, own):
        block = 2 * source_chip(way, t) + k
        return pltpu.make_async_remote_copy(
            src_ref=x.at[lats(q)] if own else band.at[lats(q), block],
            dst_ref=band.at[lats(q), block],
            send_sem=pair_send.at[way, q, t],
            recv_sem=pair_recv.at[way, q, t],
            device_id=(r, 2 * z + 1 - k),
            device_id_type=MESH,
        )

    def ring(turn, way, q, t, root):
        chip = source_chip(way, t)
        first = (q - k * mine) * tile_lats + turn * part
        here = panel.at[pl.ds(first, part), pl.ds(2 * chip, 2)]
        origin = band.at[pl.ds(q * tile_lats + turn * part, part), pl.ds(2 * chip, 2)]
        return pltpu.make_async_remote_copy(
            src_ref=origin if root else here,
            dst_ref=here,
            send_sem=ring_send.at[turn, way, q, t],
            recv_sem=ring_recv.at[turn, way, q, t],
            device_id=(ring_to[turn], c),
            device_id_type=MESH,
        )

    def root_copy(way, q, t):
        chip = source_chip(way, t)
        return pltpu.make_async_copy(
            band.at[lats(q), pl.ds(2 * chip, 2)],
            panel.at[pl.ds((q - k * mine) * tile_lats, tile_lats), pl.ds(2 * chip, 2)],
            root_sem.at[way, q, t],
        )

    def chain_slot(i):
        q, t = slot_of(i)

        @pl.when(t == 0)
        def _():
            local(q).start()
            for way in range(2):
                @pl.when(has_next[way])
                def _(way=way):
                    chain(way, q, 0, True).start()
            pair(0, q, 0, True).start()

        for way in range(2):
            @pl.when(jnp.logical_and(t > 0, valid(way, t)))
            def _(way=way):
                chain(way, q, t - 1, False).wait_recv()

                @pl.when(has_next[way])
                def _():
                    chain(way, q, t, False).start()
                pair(way, q, t, False).start()

    def used(way, q, t):
        return jnp.logical_and(valid(way, t), q // mine == k)

    def root_slot(i):
        q, t = slot_of(i)
        for way in range(2):
            @pl.when(valid(way, t))
            def _(way=way):
                pair(way, q, t, False).wait_recv()

                @pl.when(jnp.logical_and(way == 0, t == 0))
                def _():
                    local(q).wait()

                @pl.when(q // mine == k)
                def _():
                    for turn in range(2):
                        ring(turn, way, q, t, True).start()
                    root_copy(way, q, t).start()

    def leaf_slot(i):
        q, t = slot_of(i)
        for way in range(2):
            @pl.when(used(way, q, t))
            def _(way=way):
                for turn in range(2):
                    ring(turn, way, q, t, False).wait_recv()

                    @pl.when(hops[turn] < rows - 1)
                    def _(turn=turn):
                        ring(turn, way, q, t, False).start()

    @pl.loop(0, slots + lag)
    def _(i):
        @pl.when(i < slots)
        def _():
            chain_slot(i)

            @pl.when(is_root)
            def _():
                root_slot(i)

        @pl.when(jnp.logical_and(i >= lag, jnp.logical_not(is_root)))
        def _():
            leaf_slot(i - lag)

    @pl.loop(0, slots)
    def _(i):
        q, t = slot_of(i)

        @pl.when(jnp.logical_and(t == 0, jnp.logical_not(is_root)))
        def _():
            local(q).wait()

        for way in range(2):
            @pl.when(jnp.logical_and(has_next[way], jnp.logical_or(valid(way, t), t == 0)))
            def _(way=way):
                chain(way, q, t, False).wait_send()

            @pl.when(valid(way, t))
            def _(way=way):
                pair(way, q, t, False).wait_send()

                @pl.when(jnp.logical_not(is_root))
                def _():
                    pair(way, q, t, False).wait_recv()

            @pl.when(used(way, q, t))
            def _(way=way):
                for turn in range(2):
                    @pl.when(jnp.logical_or(is_root, hops[turn] < rows - 1))
                    def _(turn=turn):
                        ring(turn, way, q, t, False).wait_send()

                @pl.when(is_root)
                def _():
                    root_copy(way, q, t).wait()


def gather(block, tile_lats, panel_lats):
    rows, cols = lax.axis_size("row"), lax.axis_size("col")
    chips = cols // 2
    lat_rows, lon_cols, maps = block.shape
    tiles = lat_rows // tile_lats
    sems = pltpu.SemaphoreType.DMA
    hbm = pl.BlockSpec(memory_space=pltpu.HBM)
    return pl.pallas_call(
        functools.partial(gather_kernel, rows, chips, tile_lats),
        out_shape=(
            jax.ShapeDtypeStruct((lat_rows, cols, lon_cols, maps), block.dtype),
            jax.ShapeDtypeStruct((panel_lats, cols, lon_cols, maps), block.dtype),
        ),
        in_specs=[hbm],
        out_specs=(hbm, hbm),
        scratch_shapes=[
            sems((tiles,)),
            sems((2, tiles, chips)),
            sems((2, tiles, chips)),
            sems((2, tiles, chips)),
            sems((2, tiles, chips)),
            sems((2, tiles, chips)),
            sems((2, 2, tiles, chips)),
            sems((2, 2, tiles, chips)),
        ],
        compiler_params=pltpu.CompilerParams(collective_id=0, has_side_effects=True),
        name="gather_maps",
    )(block)


def product_kernel(row_tile_count, col_tile_count, strip, wide, left, right, out):
    row = lax.axis_index("row") * row_tile_count + pl.program_id(0) * strip // TILE
    first_col = lax.axis_index("col") * col_tile_count
    scale = 1.0 / left.shape[1]

    @pl.loop(0, out.shape[1] // wide)
    def _(j):
        at = pl.ds(pl.multiple_of(j * wide, wide), wide)
        keep = first_col + j * wide // TILE >= row

        @pl.when(keep)
        def _():
            acc = lax.dot_general(
                left[...], right[at, :], (((1,), (1,)), ((), ())),
                preferred_element_type=jnp.float32)
            out[:, at] = (acc * scale).astype(out.dtype)

        @pl.when(jnp.logical_not(keep))
        def _():
            out[:, at] = jnp.zeros((out.shape[0], wide), out.dtype)


def product(left, right):
    rows, maps = left.shape
    cols = right.shape[0]
    strip, wide = 512, 1024
    return pl.pallas_call(
        functools.partial(product_kernel, rows // TILE, cols // TILE, strip, wide),
        grid=(rows // strip,),
        out_shape=jax.ShapeDtypeStruct((rows, cols), jnp.bfloat16),
        in_specs=[
            pl.BlockSpec((strip, maps), lambda i: (i, 0)),
            pl.BlockSpec((cols, maps), lambda i: (0, 0)),
        ],
        out_specs=pl.BlockSpec((strip, cols), lambda i: (i, 0)),
        compiler_params=pltpu.CompilerParams(vmem_limit_bytes=VMEM_LIMIT),
        name="covariance_product",
    )(left, right)


def per_device(anomalies, kappa, members, months, land):
    lat_rows, lon_cols, maps = anomalies.shape
    row_index = lax.axis_index("row")
    lat_ids = row_index * lat_rows + jnp.arange(lat_rows, dtype=jnp.int32)
    phi = ((lat_ids.astype(jnp.float32) + 0.5) / LAT - 0.5) * math.pi
    lat_weight = jnp.sqrt(jnp.cos(phi))
    sea_weight = jnp.where(land == 1, 1.0, 0.5).astype(jnp.float32)
    cell_weight = sea_weight * lat_weight[:, None]
    groups = members * MONTHS + months
    onehot = (groups[:, None] == jnp.arange(GROUPS, dtype=jnp.int32)[None, :]).astype(jnp.float32)
    counts = jnp.maximum(jnp.sum(onehot, axis=0), 1.0)
    field = extended(anomalies, "col", 1, STEPS, True)
    field = extended(field, "row", 0, STEPS, False).astype(jnp.float32)
    coeff = extended(extended(kappa, "col", 1, STEPS, True), "row", 0, STEPS, False)
    coeff = coeff.astype(jnp.float32)[:, :, None]
    for step in range(STEPS):
        inner = field[1:-1, 1:-1]
        coeff = coeff[1:-1, 1:-1]
        beside = field[2:, 1:-1] + field[:-2, 1:-1] + (field[1:-1, 2:] + field[1:-1, :-2])
        field = inner + coeff * (beside - 4.0 * inner)
    block = centre_maps(field, cell_weight, onehot, counts)
    lon = lon_cols * lax.axis_size("col")
    panel_lats = lat_rows * lax.axis_size("row") // lax.axis_size("col")
    band, panel = gather(block, TILE // lon, panel_lats)
    return product(band.reshape(-1, maps), panel.reshape(-1, maps))


def solution(mesh):
    placed = (P("row", "col", None), P("row", "col"), P(), P(), P("row", "col"))
    return jax.shard_map(
        per_device, mesh=mesh, in_specs=placed, out_specs=P("row", "col"), check_vma=False
    )
```

time: 515 us -> 643 us (1.25); the launches traced: 514 us -> 630 us
  Pallas kernels: 0 us -> 577 us
  waiting for transfers between devices: 331 us -> 10.6 us
  matrix products: 84.5 us -> 5.33 us
  starting transfers between devices: 39.7 us -> 14.9 us
  other arithmetic: 39.1 us -> 19.3 us
  between operations: 13.9 us -> 0.12 us
    pallas_call x0 -> x2, Pallas kernels: none -> 577 us  [the longest x1 497 us: gather(): pl.pallas_call(functools.partial(gather_kernel, rows, chips, tile_lats),...]
    psum x1 -> x0, waiting for transfers between devices: 170 us -> none  [from_root(): return lax.psum(jnp.where(mine, array, jnp.zeros_like(array)), axis)]
    all_gather x1 -> x0, waiting for transfers between devices: 157 us -> none  [per_device(): band = lax.all_gather(block, 'col', axis=1, tiled=True)]
    dot_general x1 -> x0, matrix products: 78.6 us -> none  [per_device(): lax.dot_general(left, right, (((1,), (1,)), ((), ())), preferred_element_...]
    ppermute x8 -> x4, starting transfers between devices: 28.1 us -> 12.1 us  [extended(): before = lax.ppermute(last, axis, up)]
    add x4, other arithmetic: 27.4 us -> 13.5 us  [per_device(): field = inner + coeff * (beside - 4.0 * inner)]
    ppermute x8 -> x4, starting transfers between devices: 11.4 us -> 2.82 us  [extended(): after = lax.ppermute(first, axis, down)]
    ppermute x8 -> x4, waiting for transfers between devices: 0.02 us -> 8.08 us  [extended(): after = lax.ppermute(first, axis, down)]
  transfers between devices with their start and end apart: 18 -> 8, of which waited for: 5 -> 3; matrix products, arithmetic and copies ran while one was open for 1% -> 1% of each run, Pallas kernels for 0% -> 0%
where the time goes in v1:
time: 643 us; the launch traced here: 630 us
  Pallas kernels  577 us (90%)
  other arithmetic  19.3 us (3%)
  starting transfers between devices  14.9 us (2%)
  waiting for transfers between devices  10.6 us (2%)
    pallas_call x1, Pallas kernels, gather(): pl.pallas_call(functools.partial(gather_kernel, rows, chips, tile_lats),...  497 us
    pallas_call x1, Pallas kernels, product(): pl.pallas_call(functools.partial(product_kernel, rows // TILE, cols // TI...  79.7 us
    add x4, other arithmetic, per_device(): field = inner + coeff * (beside - 4.0 * inner)  13.5 us
  transfers between devices with their start and end apart: 8, of which 3 were waited for; matrix products, arithmetic and copies ran while one was open for 1% of the time, Pallas kernels for 0%

profile of v1, /device:TPU:1, one launch (start us, length us, event | category | flops | bytes accessed | tf_op | source)
XLA Modules:
  0.0 630.2 jit_solution(6803022741655702896)
XLA Ops:
  0.0 0.9 fusion.20
  0.9 2.7 collective-permute-start.4
  3.6 1.4 fusion.18
  5.0 1.8 collective-permute-start
  6.8 0.2 collective-permute-start.1
  7.1 0.7 multiply_add_fusion
  7.8 0.1 convert_reduce_fusion
  8.0 0.8 select_multiply_fusion
  8.8 0.1 mul.128
  8.8 0.8 pad_maximum_fusion.3
  9.6 3.6 collective-permute-start.6
  13.2 1.3 collective-permute-start.7
  14.5 0.8 fusion.23
  15.3 2.2 collective-permute-done.7
  17.5 0.1 slice_bitcast_fusion
  17.6 0.1 slice_bitcast_fusion.1
  17.7 1.3 pad_maximum_fusion.2
  19.0 4.0 collective-permute-start.2
  23.0 1.3 collective-permute-start.3
  24.3 0.1 slice_bitcast_fusion.3
  24.4 0.1 slice_bitcast_fusion.2
  24.4 2.5 collective-permute-done.2
  27.0 5.8 collective-permute-done.3
  32.8 1.3 maximum_convert_fusion
  34.1 3.8 fusion.3
  37.9 3.6 fusion.7
  41.5 3.4 fusion.11
  45.0 2.7 fusion.15
  47.6 2.1 convolution_divide_fusion
  49.7 3.3 multiply_convert_fusion
  53.0 497.5 %gather_maps.1 = (bf16[32,8,32,1024]{3,2,1,0:T(8,128)(2,1)}, bf16[16,8,32,1024]{3,2,1,0:T(8,128)(2,1)}) custom-call(bf16[32,32,1024]{2,1,0:T(8,128)(2,1)} %bitcast.21), custom_call_target="tpu_custom_call" | custom-call | tf_op jit(solution)/shard_map/gather_maps/pallas_call | solution.py:255
  550.5 79.7 %covariance_product.1 = bf16[8192,4096]{1,0:T(8,128)(2,1)} custom-call(bf16[8192,1024]{1,0:T(8,128)(2,1)} %bitcast.20, bf16[4096,1024]{1,0:T(8,128)(2,1)} %bitcast.22), custom_call_target="tpu_custom_call" | custom-call | tf_op jit(solution)/shard_map/covariance_product/pallas_call | solution.py:304
  (12 shorter events, 0.1 us)
Async XLA Ops:
  0.0 32.8 %copy-start = (bf16[32,32,1024]{2,1,0:T(8,128)(2,1)S(1)}, bf16[32,32,1024]{2,1,0:T(8,128)(2,1)}, u32[]{:S(2)}) copy-start(bf16[32,32,1024]{2,1,0:T(8,128)(2,1)} %param.5) | copy-start | bytes 6291460
  0.9 7.9 %collective-permute-start.4 = (bf16[32,4]{1,0:T(8,128)(2,1)S(1)}, bf16[32,4]{1,0:T(8,128)(2,1)S(1)}, u32[]{:S(2)}, u32[]{:S(2)}) collective-permute-start(bf16[32,4]{1,0:T(8,128)(2,1)S(1)} %get-tuple-element.15), channel_id=1, source_target_pairs={{0,1},{1,2},{2,3},{3,4},{4,5},{5,6},{6,7},{7,0},{8,9},{9,10},{10,1... | collective-permute-start | bytes 776 | tf_op jit(solution)/shard_map/ppermute | solution.py:26
  3.6 5.2 collective-permute-start.5
  5.0 12.6 %collective-permute-start = (bf16[32,4,1024]{2,1,0:T(4,128)(2,1)S(1)}, bf16[32,4,1024]{2,1,0:T(4,128)(2,1)S(1)}, u32[]{:S(2)}, u32[]{:S(2)}) collective-permute-start(bf16[32,4,1024]{2,1,0:T(4,128)(2,1)S(1)} %get-tuple-element.11), channel_id=1, source_target_pairs={{0,1},{1,2},{2,3},{3,4},{4,5},{5,6},{6,7},{7,0},{8,9},{9,10},{10,1... | collective-permute-start | bytes 786440 | tf_op jit(solution)/shard_map/ppermute | solution.py:26
  6.8 10.8 %collective-permute-start.1 = (bf16[32,4,1024]{2,1,0:T(4,128)(2,1)S(1)}, bf16[32,4,1024]{2,1,0:T(4,128)(2,1)S(1)}, u32[]{:S(2)}, u32[]{:S(2)}) collective-permute-start(bf16[32,4,1024]{2,1,0:T(4,128)(2,1)S(1)} %get-tuple-element.12), channel_id=1, source_target_pairs={{1,0},{2,1},{3,2},{4,3},{5,4},{6,5},{7,6},{0,7},{9,8},{10,9},{11,1... | collective-permute-start | bytes 786440 | tf_op jit(solution)/shard_map/ppermute | solution.py:27
  9.6 5.7 collective-permute-start.6
  13.2 4.3 collective-permute-start.7
  19.0 8.0 %collective-permute-start.2 = (bf16[4,40,1024]{2,1,0:T(8,128)(2,1)S(1)}, bf16[4,40,1024]{2,1,0:T(8,128)(2,1)S(1)}, u32[]{:S(2)}, u32[]{:S(2)}) collective-permute-start(bf16[4,40,1024]{2,1,0:T(8,128)(2,1)S(1)} %get-tuple-element.9), channel_id=1, source_target_pairs={{0,8},{8,16},{16,24},{1,9},{9,17},{17,25},{2,10},{10,18},{18,26},{... | collective-permute-start | bytes 983048 | tf_op jit(solution)/shard_map/ppermute | solution.py:26
  23.0 9.8 %collective-permute-start.3 = (bf16[4,40,1024]{2,1,0:T(8,128)(2,1)S(1)}, bf16[4,40,1024]{2,1,0:T(8,128)(2,1)S(1)}, u32[]{:S(2)}, u32[]{:S(2)}) collective-permute-start(bf16[4,40,1024]{2,1,0:T(8,128)(2,1)S(1)} %get-tuple-element.10), channel_id=1, source_target_pairs={{8,0},{16,8},{24,16},{9,1},{17,9},{25,17},{10,2},{18,10},{26,18},{... | collective-permute-start | bytes 983048 | tf_op jit(solution)/shard_map/ppermute | solution.py:27

commit v2 on v1

--- a/solution.py
+++ b/solution.py
@@ -59,7 +59,7 @@
     mine = tiles // 2
     part = tile_lats // 2
     slots = tiles * chips
-    lag = 2
+    spread = 2
     place, _ = ring_place(r, rows)
     root_place, _ = ring_place(z, rows)
     ring_to = (ring_row(place + 1, rows), ring_row(place - 1, rows))
@@ -186,31 +186,36 @@
                         ring(turn, way, q, t, True).start()
                     root_copy(way, q, t).start()
 
-    def leaf_slot(i):
+    def leaf_slot(turn, i):
         q, t = slot_of(i)
         for way in range(2):
             @pl.when(used(way, q, t))
             def _(way=way):
-                for turn in range(2):
-                    ring(turn, way, q, t, False).wait_recv()
-
-                    @pl.when(hops[turn] < rows - 1)
-                    def _(turn=turn):
-                        ring(turn, way, q, t, False).start()
-
-    @pl.loop(0, slots + lag)
+                ring(turn, way, q, t, False).wait_recv()
+
+                @pl.when(hops[turn] < rows - 1)
+                def _():
+                    ring(turn, way, q, t, False).start()
+
+    def within(i):
+        return jnp.logical_and(i >= 0, i < slots)
+
+    @pl.loop(0, slots + spread * (rows - 1))
     def _(i):
         @pl.when(i < slots)
         def _():
             chain_slot(i)
 
-            @pl.when(is_root)
-            def _():
-                root_slot(i)
-
-        @pl.when(jnp.logical_and(i >= lag, jnp.logical_not(is_root)))
+        @pl.when(jnp.logical_and(is_root, within(i - 1)))
         def _():
-            leaf_slot(i - lag)
+            root_slot(i - 1)
+
+        for turn in range(2):
+            late = i - spread * hops[turn]
+
+            @pl.when(jnp.logical_and(jnp.logical_not(is_root), within(late)))
+            def _(turn=turn, late=late):
+                leaf_slot(turn, late)
 
     @pl.loop(0, slots)
     def _(i):
@@ -275,41 +280,42 @@
     )(block)
 
 
-def product_kernel(row_tile_count, col_tile_count, strip, wide, left, right, out):
+def product_kernel(row_tile_count, col_tile_count, wide, left, right, out):
+    strip, part = out.shape
     row = lax.axis_index("row") * row_tile_count + pl.program_id(0) * strip // TILE
-    first_col = lax.axis_index("col") * col_tile_count
+    col = lax.axis_index("col") * col_tile_count + pl.program_id(1) * part // TILE
+    keep = col >= row
     scale = 1.0 / left.shape[1]
 
-    @pl.loop(0, out.shape[1] // wide)
-    def _(j):
-        at = pl.ds(pl.multiple_of(j * wide, wide), wide)
-        keep = first_col + j * wide // TILE >= row
-
-        @pl.when(keep)
-        def _():
+    @pl.when(keep)
+    def _():
+        @pl.loop(0, part // wide)
+        def _(j):
+            to = pl.ds(pl.multiple_of(j * wide, wide), wide)
+            at = pl.ds(pl.multiple_of(pl.program_id(1) * part + j * wide, wide), wide)
             acc = lax.dot_general(
                 left[...], right[at, :], (((1,), (1,)), ((), ())),
                 preferred_element_type=jnp.float32)
-            out[:, at] = (acc * scale).astype(out.dtype)
-
-        @pl.when(jnp.logical_not(keep))
-        def _():
-            out[:, at] = jnp.zeros((out.shape[0], wide), out.dtype)
+            out[:, to] = (acc * scale).astype(out.dtype)
+
+    @pl.when(jnp.logical_not(keep))
+    def _():
+        out[...] = jnp.zeros_like(out)
 
 
 def product(left, right):
     rows, maps = left.shape
     cols = right.shape[0]
-    strip, wide = 512, 1024
+    strip, part, wide = TILE // 2, TILE, TILE // 4
     return pl.pallas_call(
-        functools.partial(product_kernel, rows // TILE, cols // TILE, strip, wide),
-        grid=(rows // strip,),
+        functools.partial(product_kernel, rows // TILE, cols // TILE, wide),
+        grid=(rows // strip, cols // part),
         out_shape=jax.ShapeDtypeStruct((rows, cols), jnp.bfloat16),
         in_specs=[
-            pl.BlockSpec((strip, maps), lambda i: (i, 0)),
-            pl.BlockSpec((cols, maps), lambda i: (0, 0)),
+            pl.BlockSpec((strip, maps), lambda i, j: (i, 0)),
+            pl.BlockSpec((cols, maps), lambda i, j: (0, 0), pipeline_mode=pl.Buffered(1)),
         ],
-        out_specs=pl.BlockSpec((strip, cols), lambda i: (i, 0)),
+        out_specs=pl.BlockSpec((strip, part), lambda i, j: (i, j)),
         compiler_params=pltpu.CompilerParams(vmem_limit_bytes=VMEM_LIMIT),
         name="covariance_product",
     )(left, right)

time: 643 us -> 505 us (0.79); the launches traced: 630 us -> 501 us
  Pallas kernels: 577 us -> 448 us
    pallas_call x1, Pallas kernels: 497 us -> 365 us  [gather(): pl.pallas_call(functools.partial(gather_kernel, rows, chips, tile_lats),...]
where the time goes in v2:
time: 505 us; the launch traced here: 501 us
  Pallas kernels  448 us (89%)
  other arithmetic  19.3 us (4%)
  starting transfers between devices  14.9 us (3%)
  waiting for transfers between devices  10.6 us (2%)
  matrix products  5.33 us (1%)
    pallas_call x1, Pallas kernels, gather(): pl.pallas_call(functools.partial(gather_kernel, rows, chips, tile_lats),...  365 us
    pallas_call x1, Pallas kernels, product(): pl.pallas_call(functools.partial(product_kernel, rows // TILE, cols // TI...  82.9 us
    add x4, other arithmetic, per_device(): field = inner + coeff * (beside - 4.0 * inner)  13.5 us
    ppermute x4, starting transfers between devices, extended(): before = lax.ppermute(last, axis, up)  12.1 us
  transfers between devices with their start and end apart: 8, of which 3 were waited for; matrix products, arithmetic and copies ran while one was open for 1% of the time, Pallas kernels for 0%

profile of v2, /device:TPU:1, one launch (start us, length us, event | category | flops | bytes accessed | tf_op | source)
XLA Modules:
  0.0 501.2 jit_solution(17902197571496674838)
XLA Ops:
  0.0 0.9 fusion.20
  0.9 2.7 collective-permute-start.4
  3.6 1.4 fusion.18
  5.0 1.8 collective-permute-start
  6.8 0.2 collective-permute-start.1
  7.1 0.7 multiply_add_fusion
  7.8 0.1 convert_reduce_fusion
  8.0 0.8 select_multiply_fusion
  8.8 0.1 mul.128
  8.8 0.8 pad_maximum_fusion.3
  9.6 3.6 collective-permute-start.6
  13.2 1.3 collective-permute-start.7
  14.5 0.8 fusion.23
  15.3 2.2 collective-permute-done.7
  17.5 0.1 slice_bitcast_fusion
  17.6 0.1 slice_bitcast_fusion.1
  17.7 1.3 pad_maximum_fusion.2
  19.0 4.0 collective-permute-start.2
  23.0 1.3 collective-permute-start.3
  24.3 0.1 slice_bitcast_fusion.3
  24.4 0.1 slice_bitcast_fusion.2
  24.4 2.5 collective-permute-done.2
  27.0 5.8 %collective-permute-done.3 = bf16[4,40,1024]{2,1,0:T(8,128)(2,1)S(1)} collective-permute-done((bf16[4,40,1024]{2,1,0:T(8,128)(2,1)S(1)}, bf16[4,40,1024]{2,1,0:T(8,128)(2,1)S(1)}, u32[]{:S(2)}, u32[]{:S(2)}) %collective-permute-start.3) | collective-permute-done | bytes 327712 | tf_op jit(solution)/shard_map/ppermute | solution.py:27
  32.8 1.3 maximum_convert_fusion
  34.1 3.8 fusion.3
  37.9 3.6 fusion.7
  41.5 3.4 fusion.11
  45.0 2.7 fusion.15
  47.6 2.1 convolution_divide_fusion
  49.7 3.3 multiply_convert_fusion
  53.0 365.3 %gather_maps.1 = (bf16[32,8,32,1024]{3,2,1,0:T(8,128)(2,1)}, bf16[16,8,32,1024]{3,2,1,0:T(8,128)(2,1)}) custom-call(bf16[32,32,1024]{2,1,0:T(8,128)(2,1)} %bitcast.21), custom_call_target="tpu_custom_call" | custom-call | tf_op jit(solution)/shard_map/gather_maps/pallas_call | solution.py:260
  418.3 82.9 %covariance_product.1 = bf16[8192,4096]{1,0:T(8,128)(2,1)} custom-call(bf16[8192,1024]{1,0:T(8,128)(2,1)} %bitcast.20, bf16[4096,1024]{1,0:T(8,128)(2,1)} %bitcast.22), custom_call_target="tpu_custom_call" | custom-call | tf_op jit(solution)/shard_map/covariance_product/pallas_call | solution.py:310
  (12 shorter events, 0.1 us)
Async XLA Ops:
  0.0 32.8 %copy-start = (bf16[32,32,1024]{2,1,0:T(8,128)(2,1)S(1)}, bf16[32,32,1024]{2,1,0:T(8,128)(2,1)}, u32[]{:S(2)}) copy-start(bf16[32,32,1024]{2,1,0:T(8,128)(2,1)} %param.5) | copy-start | bytes 6291460
  0.9 7.9 %collective-permute-start.4 = (bf16[32,4]{1,0:T(8,128)(2,1)S(1)}, bf16[32,4]{1,0:T(8,128)(2,1)S(1)}, u32[]{:S(2)}, u32[]{:S(2)}) collective-permute-start(bf16[32,4]{1,0:T(8,128)(2,1)S(1)} %get-tuple-element.15), channel_id=1, source_target_pairs={{0,1},{1,2},{2,3},{3,4},{4,5},{5,6},{6,7},{7,0},{8,9},{9,10},{10,1... | collective-permute-start | bytes 776 | tf_op jit(solution)/shard_map/ppermute | solution.py:26
  3.6 5.2 %collective-permute-start.5 = (bf16[32,4]{1,0:T(8,128)(2,1)S(1)}, bf16[32,4]{1,0:T(8,128)(2,1)S(1)}, u32[]{:S(2)}, u32[]{:S(2)}) collective-permute-start(bf16[32,4]{1,0:T(8,128)(2,1)S(1)} %get-tuple-element.16), channel_id=1, source_target_pairs={{1,0},{2,1},{3,2},{4,3},{5,4},{6,5},{7,6},{0,7},{9,8},{10,9},{11,1... | collective-permute-start | bytes 776 | tf_op jit(solution)/shard_map/ppermute | solution.py:27
  5.0 12.6 %collective-permute-start = (bf16[32,4,1024]{2,1,0:T(4,128)(2,1)S(1)}, bf16[32,4,1024]{2,1,0:T(4,128)(2,1)S(1)}, u32[]{:S(2)}, u32[]{:S(2)}) collective-permute-start(bf16[32,4,1024]{2,1,0:T(4,128)(2,1)S(1)} %get-tuple-element.11), channel_id=1, source_target_pairs={{0,1},{1,2},{2,3},{3,4},{4,5},{5,6},{6,7},{7,0},{8,9},{9,10},{10,1... | collective-permute-start | bytes 786440 | tf_op jit(solution)/shard_map/ppermute | solution.py:26
  6.8 10.8 %collective-permute-start.1 = (bf16[32,4,1024]{2,1,0:T(4,128)(2,1)S(1)}, bf16[32,4,1024]{2,1,0:T(4,128)(2,1)S(1)}, u32[]{:S(2)}, u32[]{:S(2)}) collective-permute-start(bf16[32,4,1024]{2,1,0:T(4,128)(2,1)S(1)} %get-tuple-element.12), channel_id=1, source_target_pairs={{1,0},{2,1},{3,2},{4,3},{5,4},{6,5},{7,6},{0,7},{9,8},{10,9},{11,1... | collective-permute-start | bytes 786440 | tf_op jit(solution)/shard_map/ppermute | solution.py:27
  9.6 5.7 %collective-permute-start.6 = (bf16[4,40]{1,0:T(4,128)(2,1)S(1)}, bf16[4,40]{1,0:T(4,128)(2,1)S(1)}, u32[]{:S(2)}, u32[]{:S(2)}) collective-permute-start(bf16[4,40]{1,0:T(4,128)(2,1)S(1)} %get-tuple-element.13), channel_id=1, source_target_pairs={{0,8},{8,16},{16,24},{1,9},{9,17},{17,25},{2,10},{10,18},{18,26},{... | collective-permute-start | bytes 968 | tf_op jit(solution)/shard_map/ppermute | solution.py:26
  13.2 4.3 collective-permute-start.7
  19.0 8.0 %collective-permute-start.2 = (bf16[4,40,1024]{2,1,0:T(8,128)(2,1)S(1)}, bf16[4,40,1024]{2,1,0:T(8,128)(2,1)S(1)}, u32[]{:S(2)}, u32[]{:S(2)}) collective-permute-start(bf16[4,40,1024]{2,1,0:T(8,128)(2,1)S(1)} %get-tuple-element.9), channel_id=1, source_target_pairs={{0,8},{8,16},{16,24},{1,9},{9,17},{17,25},{2,10},{10,18},{18,26},{... | collective-permute-start | bytes 983048 | tf_op jit(solution)/shard_map/ppermute | solution.py:26
  23.0 9.8 %collective-permute-start.3 = (bf16[4,40,1024]{2,1,0:T(8,128)(2,1)S(1)}, bf16[4,40,1024]{2,1,0:T(8,128)(2,1)S(1)}, u32[]{:S(2)}, u32[]{:S(2)}) collective-permute-start(bf16[4,40,1024]{2,1,0:T(8,128)(2,1)S(1)} %get-tuple-element.10), channel_id=1, source_target_pairs={{8,0},{16,8},{24,16},{9,1},{17,9},{25,17},{10,2},{18,10},{26,18},{... | collective-permute-start | bytes 983048 | tf_op jit(solution)/shard_map/ppermute | solution.py:27

commit v3 on v2

--- a/solution.py
+++ b/solution.py
@@ -14,7 +14,6 @@
 TILE = 2048
 GROUPS = 96
 MESH = pl.DeviceIdType.MESH
-VMEM_LIMIT = 56 * 1024 * 1024
 
 
 def extended(array, axis, dim, width, wrap):
@@ -83,8 +82,8 @@
         barrier, 3 + has_next[0].astype(jnp.int32) + has_next[1].astype(jnp.int32))
 
     def slot_of(i):
-        j = i // chips
-        return (j % 2) * mine + j // 2, i % chips
+        j = i % tiles
+        return (j % 2) * mine + j // 2, i // tiles
 
     def lats(q):
         return pl.ds(q * tile_lats, tile_lats)
@@ -100,33 +99,32 @@
     def local(q):
         return pltpu.make_async_copy(x.at[lats(q)], band.at[lats(q), c], local_sem.at[q])
 
-    def chain(way, q, t, own):
+    def block_copy(way, q, t, own, sems, target, piece):
         block = 2 * source_chip(way, t) + k
+        first, count = piece
+        at = pl.ds(q * tile_lats + first, count)
         return pltpu.make_async_remote_copy(
-            src_ref=x.at[lats(q)] if own else band.at[lats(q), block],
-            dst_ref=band.at[lats(q), block],
-            send_sem=chain_send.at[way, q, t],
-            recv_sem=chain_recv.at[way, q, t],
-            device_id=(r, c + 2 * step[way]),
+            src_ref=x.at[at] if own else band.at[at, block],
+            dst_ref=band.at[at, block],
+            send_sem=sems[0].at[way, q, t],
+            recv_sem=sems[1].at[way, q, t],
+            device_id=(r, target),
             device_id_type=MESH,
         )
 
-    def pair(way, q, t, own):
-        block = 2 * source_chip(way, t) + k
-        return pltpu.make_async_remote_copy(
-            src_ref=x.at[lats(q)] if own else band.at[lats(q), block],
-            dst_ref=band.at[lats(q), block],
-            send_sem=pair_send.at[way, q, t],
-            recv_sem=pair_recv.at[way, q, t],
-            device_id=(r, 2 * z + 1 - k),
-            device_id_type=MESH,
-        )
-
-    def ring(turn, way, q, t, root):
+    def chain(way, q, t, own=False, piece=(0, tile_lats)):
+        sems = (chain_send, chain_recv)
+        return block_copy(way, q, t, own, sems, c + 2 * step[way], piece)
+
+    def pair(way, q, t, own=False, piece=(0, tile_lats)):
+        return block_copy(way, q, t, own, (pair_send, pair_recv), 2 * z + 1 - k, piece)
+
+    def ring(turn, way, q, t, root=False, piece=(0, part)):
         chip = source_chip(way, t)
-        first = (q - k * mine) * tile_lats + turn * part
-        here = panel.at[pl.ds(first, part), pl.ds(2 * chip, 2)]
-        origin = band.at[pl.ds(q * tile_lats + turn * part, part), pl.ds(2 * chip, 2)]
+        first, count = piece
+        inside = turn * part + first
+        here = panel.at[pl.ds((q - k * mine) * tile_lats + inside, count), pl.ds(2 * chip, 2)]
+        origin = band.at[pl.ds(q * tile_lats + inside, count), pl.ds(2 * chip, 2)]
         return pltpu.make_async_remote_copy(
             src_ref=origin if root else here,
             dst_ref=here,
@@ -136,6 +134,10 @@
             device_id_type=MESH,
         )
 
+    def send(copy, size, *where):
+        for first in range(size):
+            copy(*where, piece=(first, 1)).start()
+
     def root_copy(way, q, t):
         chip = source_chip(way, t)
         return pltpu.make_async_copy(
@@ -153,8 +155,8 @@
             for way in range(2):
                 @pl.when(has_next[way])
                 def _(way=way):
-                    chain(way, q, 0, True).start()
-            pair(0, q, 0, True).start()
+                    send(chain, tile_lats, way, q, 0, True)
+            send(pair, tile_lats, 0, q, 0, True)
 
         for way in range(2):
             @pl.when(jnp.logical_and(t > 0, valid(way, t)))
@@ -163,8 +165,8 @@
 
                 @pl.when(has_next[way])
                 def _():
-                    chain(way, q, t, False).start()
-                pair(way, q, t, False).start()
+                    send(chain, tile_lats, way, q, t, False)
+                send(pair, tile_lats, way, q, t, False)
 
     def used(way, q, t):
         return jnp.logical_and(valid(way, t), q // mine == k)
@@ -183,7 +185,7 @@
                 @pl.when(q // mine == k)
                 def _():
                     for turn in range(2):
-                        ring(turn, way, q, t, True).start()
+                        send(ring, part, turn, way, q, t, True)
                     root_copy(way, q, t).start()
 
     def leaf_slot(turn, i):
@@ -195,7 +197,7 @@
 
                 @pl.when(hops[turn] < rows - 1)
                 def _():
-                    ring(turn, way, q, t, False).start()
+                    send(ring, part, turn, way, q, t, False)
 
     def within(i):
         return jnp.logical_and(i >= 0, i < slots)
@@ -280,45 +282,15 @@
     )(block)
 
 
-def product_kernel(row_tile_count, col_tile_count, wide, left, right, out):
-    strip, part = out.shape
-    row = lax.axis_index("row") * row_tile_count + pl.program_id(0) * strip // TILE
-    col = lax.axis_index("col") * col_tile_count + pl.program_id(1) * part // TILE
-    keep = col >= row
-    scale = 1.0 / left.shape[1]
-
-    @pl.when(keep)
-    def _():
-        @pl.loop(0, part // wide)
-        def _(j):
-            to = pl.ds(pl.multiple_of(j * wide, wide), wide)
-            at = pl.ds(pl.multiple_of(pl.program_id(1) * part + j * wide, wide), wide)
-            acc = lax.dot_general(
-                left[...], right[at, :], (((1,), (1,)), ((), ())),
-                preferred_element_type=jnp.float32)
-            out[:, to] = (acc * scale).astype(out.dtype)
-
-    @pl.when(jnp.logical_not(keep))
-    def _():
-        out[...] = jnp.zeros_like(out)
-
-
 def product(left, right):
-    rows, maps = left.shape
-    cols = right.shape[0]
-    strip, part, wide = TILE // 2, TILE, TILE // 4
-    return pl.pallas_call(
-        functools.partial(product_kernel, rows // TILE, cols // TILE, wide),
-        grid=(rows // strip, cols // part),
-        out_shape=jax.ShapeDtypeStruct((rows, cols), jnp.bfloat16),
-        in_specs=[
-            pl.BlockSpec((strip, maps), lambda i, j: (i, 0)),
-            pl.BlockSpec((cols, maps), lambda i, j: (0, 0), pipeline_mode=pl.Buffered(1)),
-        ],
-        out_specs=pl.BlockSpec((strip, part), lambda i, j: (i, j)),
-        compiler_params=pltpu.CompilerParams(vmem_limit_bytes=VMEM_LIMIT),
-        name="covariance_product",
-    )(left, right)
+    rows, cols = left.shape[0], right.shape[0]
+    row_tile = (lax.axis_index("row") * rows + jnp.arange(rows, dtype=jnp.int32)) // TILE
+    col_tile = (lax.axis_index("col") * cols + jnp.arange(cols, dtype=jnp.int32)) // TILE
+    whole = lax.dot_general(
+        left, right, (((1,), (1,)), ((), ())), preferred_element_type=jnp.float32)
+    whole = whole * (1.0 / left.shape[1])
+    whole = jnp.where(col_tile[None, :] >= row_tile[:, None], whole, 0.0)
+    return whole.astype(jnp.bfloat16)
 
 
 def per_device(anomalies, kappa, members, months, land):

time: 505 us -> 461 us (0.913)
  Pallas kernels: 448 us -> 329 us
  matrix products: 5.33 us -> 84.2 us
    pallas_call x1 -> x0, Pallas kernels: 82.9 us -> none  [product(): pl.pallas_call(functools.partial(product_kernel, rows // TILE, cols // TI...]
    dot_general x0 -> x1, matrix products: none -> 78.7 us  [product(): lax.dot_general(left, right, (((1,), (1,)), ((), ())), preferred_element_...]
    pallas_call x1, Pallas kernels: 365 us -> 329 us  [gather(): pl.pallas_call(functools.partial(gather_kernel, rows, chips, tile_lats),...]
where the time goes in v3:
time: 461 us; the launch traced here: 460 us
  Pallas kernels  329 us (71%)
  matrix products  84.2 us (18%)
  other arithmetic  19.3 us (4%)
  starting transfers between devices  14.9 us (3%)
  waiting for transfers between devices  10.6 us (2%)
    pallas_call x1, Pallas kernels, gather(): pl.pallas_call(functools.partial(gather_kernel, rows, chips, tile_lats),...  329 us
    dot_general x1, matrix products, product(): lax.dot_general(left, right, (((1,), (1,)), ((), ())), preferred_element_...  78.7 us
    add x4, other arithmetic, per_device(): field = inner + coeff * (beside - 4.0 * inner)  13.5 us
    ppermute x4, starting transfers between devices, extended(): before = lax.ppermute(last, axis, up)  12.1 us
  transfers between devices with their start and end apart: 8, of which 3 were waited for; matrix products, arithmetic and copies ran while one was open for 1% of the time, Pallas kernels for 0%

profile of v3, /device:TPU:1, one launch (start us, length us, event | category | flops | bytes accessed | tf_op | source)
XLA Modules:
  0.0 460.4 jit_solution(13652065468161065968)
XLA Ops:
  0.0 0.9 fusion.26
  0.9 2.7 collective-permute-start.4
  3.6 1.4 fusion.24
  5.0 1.8 collective-permute-start
  6.8 0.2 collective-permute-start.1
  7.1 0.7 multiply_add_fusion
  7.8 0.1 convert_reduce_fusion
  8.0 0.8 select_multiply_fusion
  8.8 0.1 mul.142
  8.9 0.8 pad_maximum_fusion.3
  9.7 3.6 collective-permute-start.6
  13.3 1.3 collective-permute-start.7
  14.6 0.8 fusion.31
  15.3 2.2 collective-permute-done.7
  17.6 0.1 slice_bitcast_fusion
  17.7 0.1 slice_bitcast_fusion.1
  17.7 1.3 pad_maximum_fusion.2
  19.0 4.0 collective-permute-start.2
  23.1 1.3 collective-permute-start.3
  24.4 0.1 slice_bitcast_fusion.3
  24.4 0.1 slice_bitcast_fusion.2
  24.5 2.5 collective-permute-done.2
  27.0 5.8 %collective-permute-done.3 = bf16[4,40,1024]{2,1,0:T(8,128)(2,1)S(1)} collective-permute-done((bf16[4,40,1024]{2,1,0:T(8,128)(2,1)S(1)}, bf16[4,40,1024]{2,1,0:T(8,128)(2,1)S(1)}, u32[]{:S(2)}, u32[]{:S(2)}) %collective-permute-start.3) | collective-permute-done | bytes 327712 | tf_op jit(solution)/shard_map/ppermute | solution.py:26
  32.9 1.3 maximum_convert_fusion
  34.2 3.8 fusion.3
  38.0 3.6 fusion.7
  41.6 3.4 fusion.11
  45.0 2.7 fusion.15
  47.7 2.0 convolution_divide_fusion
  49.7 3.4 multiply_convert_fusion
  53.2 328.6 %gather_maps.1 = (bf16[32,8,32,1024]{3,2,1,0:T(8,128)(2,1)}, bf16[16,8,32,1024]{3,2,1,0:T(8,128)(2,1)}) custom-call(bf16[32,32,1024]{2,1,0:T(8,128)(2,1)} %bitcast.22), custom_call_target="tpu_custom_call" | custom-call | tf_op jit(solution)/shard_map/gather_maps/pallas_call | solution.py:262
  381.8 78.7 %select_convert_fusion = bf16[8192,4096]{1,0:T(8,128)(2,1)} fusion(bf16[8192,1024]{1,0:T(8,128)(2,1)} %bitcast.25, bf16[4096,1024]{1,0:T(8,128)(2,1)} %bitcast.26, s32[4096]{0:T(1024)S(1)} %add_select_fusion.1, s32[8192]{0:T(1024)S(1)} %add_select_fusion), kind=kOutput, calls=%fused_computation | convolution fusion | flops 68853694464 | bytes 92323840 | tf_op jit(solution)/shard_map/dot_general | solution.py:289
  (14 shorter events, 0.1 us)
Async XLA Ops:
  0.0 32.9 %copy-start = (bf16[32,32,1024]{2,1,0:T(8,128)(2,1)S(1)}, bf16[32,32,1024]{2,1,0:T(8,128)(2,1)}, u32[]{:S(2)}) copy-start(bf16[32,32,1024]{2,1,0:T(8,128)(2,1)} %param.5) | copy-start | bytes 6291460
  0.9 8.0 %collective-permute-start.4 = (bf16[32,4]{1,0:T(8,128)(2,1)S(1)}, bf16[32,4]{1,0:T(8,128)(2,1)S(1)}, u32[]{:S(2)}, u32[]{:S(2)}) collective-permute-start(bf16[32,4]{1,0:T(8,128)(2,1)S(1)} %get-tuple-element.15), channel_id=1, source_target_pairs={{0,1},{1,2},{2,3},{3,4},{4,5},{5,6},{6,7},{7,0},{8,9},{9,10},{10,1... | collective-permute-start | bytes 776 | tf_op jit(solution)/shard_map/ppermute | solution.py:25
  3.6 5.3 %collective-permute-start.5 = (bf16[32,4]{1,0:T(8,128)(2,1)S(1)}, bf16[32,4]{1,0:T(8,128)(2,1)S(1)}, u32[]{:S(2)}, u32[]{:S(2)}) collective-permute-start(bf16[32,4]{1,0:T(8,128)(2,1)S(1)} %get-tuple-element.16), channel_id=1, source_target_pairs={{1,0},{2,1},{3,2},{4,3},{5,4},{6,5},{7,6},{0,7},{9,8},{10,9},{11,1... | collective-permute-start | bytes 776 | tf_op jit(solution)/shard_map/ppermute | solution.py:26
  5.0 12.7 %collective-permute-start = (bf16[32,4,1024]{2,1,0:T(4,128)(2,1)S(1)}, bf16[32,4,1024]{2,1,0:T(4,128)(2,1)S(1)}, u32[]{:S(2)}, u32[]{:S(2)}) collective-permute-start(bf16[32,4,1024]{2,1,0:T(4,128)(2,1)S(1)} %get-tuple-element.11), channel_id=1, source_target_pairs={{0,1},{1,2},{2,3},{3,4},{4,5},{5,6},{6,7},{7,0},{8,9},{9,10},{10,1... | collective-permute-start | bytes 786440 | tf_op jit(solution)/shard_map/ppermute | solution.py:25
  6.8 10.9 %collective-permute-start.1 = (bf16[32,4,1024]{2,1,0:T(4,128)(2,1)S(1)}, bf16[32,4,1024]{2,1,0:T(4,128)(2,1)S(1)}, u32[]{:S(2)}, u32[]{:S(2)}) collective-permute-start(bf16[32,4,1024]{2,1,0:T(4,128)(2,1)S(1)} %get-tuple-element.12), channel_id=1, source_target_pairs={{1,0},{2,1},{3,2},{4,3},{5,4},{6,5},{7,6},{0,7},{9,8},{10,9},{11,1... | collective-permute-start | bytes 786440 | tf_op jit(solution)/shard_map/ppermute | solution.py:26
  9.7 5.7 %collective-permute-start.6 = (bf16[4,40]{1,0:T(4,128)(2,1)S(1)}, bf16[4,40]{1,0:T(4,128)(2,1)S(1)}, u32[]{:S(2)}, u32[]{:S(2)}) collective-permute-start(bf16[4,40]{1,0:T(4,128)(2,1)S(1)} %get-tuple-element.13), channel_id=1, source_target_pairs={{0,8},{8,16},{16,24},{1,9},{9,17},{17,25},{2,10},{10,18},{18,26},{... | collective-permute-start | bytes 968 | tf_op jit(solution)/shard_map/ppermute | solution.py:25
  13.3 4.3 collective-permute-start.7
  19.0 8.0 %collective-permute-start.2 = (bf16[4,40,1024]{2,1,0:T(8,128)(2,1)S(1)}, bf16[4,40,1024]{2,1,0:T(8,128)(2,1)S(1)}, u32[]{:S(2)}, u32[]{:S(2)}) collective-permute-start(bf16[4,40,1024]{2,1,0:T(8,128)(2,1)S(1)} %get-tuple-element.9), channel_id=1, source_target_pairs={{0,8},{8,16},{16,24},{1,9},{9,17},{17,25},{2,10},{10,18},{18,26},{... | collective-permute-start | bytes 983048 | tf_op jit(solution)/shard_map/ppermute | solution.py:25
  23.1 9.8 %collective-permute-start.3 = (bf16[4,40,1024]{2,1,0:T(8,128)(2,1)S(1)}, bf16[4,40,1024]{2,1,0:T(8,128)(2,1)S(1)}, u32[]{:S(2)}, u32[]{:S(2)}) collective-permute-start(bf16[4,40,1024]{2,1,0:T(8,128)(2,1)S(1)} %get-tuple-element.10), channel_id=1, source_target_pairs={{8,0},{16,8},{24,16},{9,1},{17,9},{25,17},{10,2},{18,10},{26,18},{... | collective-permute-start | bytes 983048 | tf_op jit(solution)/shard_map/ppermute | solution.py:26

commit v4 on v3

--- a/solution.py
+++ b/solution.py
@@ -48,7 +48,7 @@
 
 def gather_kernel(
     rows, chips, tile_lats, x, band, panel,
-    local_sem, root_sem, chain_send, chain_recv, pair_send, pair_recv, ring_send, ring_recv,
+    local_sem, chain_send, chain_recv, pair_send, pair_recv, ring_send, ring_recv,
 ):
     r = lax.axis_index("row")
     c = lax.axis_index("col")
@@ -85,9 +85,6 @@
         j = i % tiles
         return (j % 2) * mine + j // 2, i // tiles
 
-    def lats(q):
-        return pl.ds(q * tile_lats, tile_lats)
-
     def source_chip(way, t):
         return z - step[way] * t
 
@@ -96,8 +93,10 @@
         ok = jnp.logical_and(chip >= 0, chip < chips)
         return ok if way == 0 else jnp.logical_and(ok, t > 0)
 
-    def local(q):
-        return pltpu.make_async_copy(x.at[lats(q)], band.at[lats(q), c], local_sem.at[q])
+    def local(q, piece=(0, tile_lats)):
+        first, count = piece
+        at = pl.ds(q * tile_lats + first, count)
+        return pltpu.make_async_copy(x.at[at], band.at[at, c], local_sem.at[q])
 
     def block_copy(way, q, t, own, sems, target, piece):
         block = 2 * source_chip(way, t) + k
@@ -138,20 +137,12 @@
         for first in range(size):
             copy(*where, piece=(first, 1)).start()
 
-    def root_copy(way, q, t):
-        chip = source_chip(way, t)
-        return pltpu.make_async_copy(
-            band.at[lats(q), pl.ds(2 * chip, 2)],
-            panel.at[pl.ds((q - k * mine) * tile_lats, tile_lats), pl.ds(2 * chip, 2)],
-            root_sem.at[way, q, t],
-        )
-
     def chain_slot(i):
         q, t = slot_of(i)
 
         @pl.when(t == 0)
         def _():
-            local(q).start()
+            send(local, tile_lats, q)
             for way in range(2):
                 @pl.when(has_next[way])
                 def _(way=way):
@@ -186,7 +177,6 @@
                 def _():
                     for turn in range(2):
                         send(ring, part, turn, way, q, t, True)
-                    root_copy(way, q, t).start()
 
     def leaf_slot(turn, i):
         q, t = slot_of(i)
@@ -246,10 +236,6 @@
                     @pl.when(jnp.logical_or(is_root, hops[turn] < rows - 1))
                     def _(turn=turn):
                         ring(turn, way, q, t, False).wait_send()
-
-                @pl.when(is_root)
-                def _():
-                    root_copy(way, q, t).wait()
 
 
 def gather(block, tile_lats, panel_lats):
@@ -269,7 +255,6 @@
         out_specs=(hbm, hbm),
         scratch_shapes=[
             sems((tiles,)),
-            sems((2, tiles, chips)),
             sems((2, tiles, chips)),
             sems((2, tiles, chips)),
             sems((2, tiles, chips)),
@@ -317,6 +302,10 @@
     lon = lon_cols * lax.axis_size("col")
     panel_lats = lat_rows * lax.axis_size("row") // lax.axis_size("col")
     band, panel = gather(block, TILE // lon, panel_lats)
+    col_index = lax.axis_index("col")
+    ratio = lax.axis_size("col") // lax.axis_size("row")
+    own_panel = lax.dynamic_slice_in_dim(band, col_index % ratio * panel_lats, panel_lats, 0)
+    panel = jnp.where(col_index // ratio == row_index, own_panel, panel)
     return product(band.reshape(-1, maps), panel.reshape(-1, maps))
 
 

time: 461 us -> 333 us (0.72)
  the two profiles are of different devices: /device:TPU:1 before, /device:TPU:3 now
where the time goes in v4:
time: 333 us; the launch traced here: 332 us
  Pallas kernels  192 us (58%)
  matrix products  84 us (25%)
  other arithmetic  28.3 us (8%)
  starting transfers between devices  14.9 us (4%)
  waiting for transfers between devices  10.5 us (3%)
    pallas_call x1, Pallas kernels, gather(): pl.pallas_call(functools.partial(gather_kernel, rows, chips, tile_lats),...  192 us
    dot_general x1, matrix products, product(): lax.dot_general(left, right, (((1,), (1,)), ((), ())), preferred_element_...  78.7 us
    add x4, other arithmetic, per_device(): field = inner + coeff * (beside - 4.0 * inner)  13.5 us
    ppermute x4, starting transfers between devices, extended(): before = lax.ppermute(last, axis, up)  8.99 us
    select_n x1, other arithmetic, per_device(): panel = jnp.where(col_index // ratio == row_index, own_panel, panel)  8.94 us
    ppermute x4, waiting for transfers between devices, extended(): after = lax.ppermute(first, axis, down)  8.11 us
  transfers between devices with their start and end apart: 8, of which 3 were waited for; matrix products, arithmetic and copies ran while one was open for 2% of the time, Pallas kernels for 0%

profile of v4, /device:TPU:3, one launch (start us, length us, event | category | flops | bytes accessed | tf_op | source)
XLA Modules:
  0.0 332.1 jit_solution(6954326346675520621)
XLA Ops:
  0.0 0.9 fusion.26
  0.9 1.9 collective-permute-start.4
  2.8 1.4 fusion.24
  4.2 1.8 collective-permute-start
  6.0 0.7 collective-permute-start.1
  6.7 0.7 multiply_add_fusion
  7.5 0.1 convert_reduce_fusion
  7.7 0.8 select_multiply_fusion
  8.4 0.1 mul.145
  8.5 0.8 pad_maximum_fusion.3
  9.3 3.1 collective-permute-start.6
  12.4 2.2 collective-permute-start.7
  14.6 0.8 fusion.31
  15.4 2.3 collective-permute-done.7
  17.7 0.1 slice_bitcast_fusion
  17.7 0.1 slice_bitcast_fusion.1
  17.8 1.3 pad_maximum_fusion.2
  19.1 2.2 collective-permute-start.2
  21.3 3.1 collective-permute-start.3
  24.4 0.1 slice_bitcast_fusion.3
  24.6 2.4 collective-permute-done.2
  26.9 5.8 %collective-permute-done.3 = bf16[4,40,1024]{2,1,0:T(8,128)(2,1)S(1)} collective-permute-done((bf16[4,40,1024]{2,1,0:T(8,128)(2,1)S(1)}, bf16[4,40,1024]{2,1,0:T(8,128)(2,1)S(1)}, u32[]{:S(2)}, u32[]{:S(2)}) %collective-permute-start.3) | collective-permute-done | bytes 327712 | tf_op jit(solution)/shard_map/ppermute | solution.py:26
  32.8 1.3 maximum_convert_fusion
  34.0 3.8 %fusion.3 = f32[38,38,1024]{2,1,0:T(8,128)S(1)} fusion(f32[40,40,1024]{2,1,0:T(8,128)S(1)} %maximum_convert_fusion, f32[38,38]{1,0:T(8,128)S(1)} %slice_bitcast_fusion.2), kind=kLoop, calls=%fused_computation.6 | loop fusion | flops 10350592 | bytes 35493520 | tf_op jit(solution)/shard_map/add | solution.py:300
  37.9 3.6 %fusion.7 = f32[36,36,1024]{2,1,0:T(8,128)S(1)} fusion(f32[38,38,1024]{2,1,0:T(8,128)S(1)} %fusion.3, f32[36,36]{1,0:T(8,128)S(1)} %slice_bitcast_fusion.1), kind=kLoop, calls=%fused_computation.12 | loop fusion | flops 9289728 | bytes 31855680 | tf_op jit(solution)/shard_map/add | solution.py:300
  41.5 3.4 %fusion.11 = f32[34,34,1024]{2,1,0:T(8,128)S(1)} fusion(f32[36,36,1024]{2,1,0:T(8,128)S(1)} %fusion.7, f32[34,34]{1,0:T(8,128)S(1)} %slice_bitcast_fusion), kind=kLoop, calls=%fused_computation.18 | loop fusion | flops 8286208 | bytes 28414480 | tf_op jit(solution)/shard_map/add | solution.py:300
  44.9 2.7 fusion.15
  47.6 2.0 convolution_divide_fusion
  49.6 3.3 multiply_convert_fusion
  52.9 191.5 %gather_maps.1 = (bf16[32,8,32,1024]{3,2,1,0:T(8,128)(2,1)}, bf16[16,8,32,1024]{3,2,1,0:T(8,128)(2,1)}) custom-call(bf16[32,32,1024]{2,1,0:T(8,128)(2,1)} %bitcast.23), custom_call_target="tpu_custom_call" | custom-call | tf_op jit(solution)/shard_map/gather_maps/pallas_call | solution.py:248
  244.5 8.9 %dynamic-slice_select_fusion = bf16[16,8,32,1024]{3,2,1,0:T(8,128)(2,1)} fusion(bf16[16,8,32,1024]{3,2,1,0:T(8,128)(2,1)} %get-tuple-element.8, bf16[32,8,32,1024]{3,2,1,0:T(8,128)(2,1)} %get-tuple-element.7, s32[]{:T(128)S(6)} %select_n.54, pred[]{:T(512)S(6)} %eq.29), kind=kLoop, calls=%fused_computation.1 | loop fusion | flops 4194304 | bytes 25165828 | tf_op jit(solution)/shard_map/jit(_where)/select_n | solution.py:308
  253.4 78.7 %select_convert_fusion = bf16[8192,4096]{1,0:T(8,128)(2,1)} fusion(bf16[8192,1024]{1,0:T(8,128)(2,1)} %bitcast.24, bf16[4096,1024]{1,0:T(8,128)(2,1)} %bitcast.22, s32[4096]{0:T(1024)S(1)} %add_select_fusion.1, s32[8192]{0:T(1024)S(1)} %add_select_fusion), kind=kOutput, calls=%fused_computation | convolution fusion | flops 68853694464 | bytes 92323840 | tf_op jit(solution)/shard_map/dot_general | solution.py:274
  (15 shorter events, 0.2 us)
Async XLA Ops:
  0.0 32.8 %copy-start = (bf16[32,32,1024]{2,1,0:T(8,128)(2,1)S(1)}, bf16[32,32,1024]{2,1,0:T(8,128)(2,1)}, u32[]{:S(2)}) copy-start(bf16[32,32,1024]{2,1,0:T(8,128)(2,1)} %param.5) | copy-start | bytes 6291460
  0.9 7.6 %collective-permute-start.4 = (bf16[32,4]{1,0:T(8,128)(2,1)S(1)}, bf16[32,4]{1,0:T(8,128)(2,1)S(1)}, u32[]{:S(2)}, u32[]{:S(2)}) collective-permute-start(bf16[32,4]{1,0:T(8,128)(2,1)S(1)} %get-tuple-element.15), channel_id=1, source_target_pairs={{0,1},{1,2},{2,3},{3,4},{4,5},{5,6},{6,7},{7,0},{8,9},{9,10},{10,1... | collective-permute-start | bytes 776 | tf_op jit(solution)/shard_map/ppermute | solution.py:25
  2.8 5.7 %collective-permute-start.5 = (bf16[32,4]{1,0:T(8,128)(2,1)S(1)}, bf16[32,4]{1,0:T(8,128)(2,1)S(1)}, u32[]{:S(2)}, u32[]{:S(2)}) collective-permute-start(bf16[32,4]{1,0:T(8,128)(2,1)S(1)} %get-tuple-element.16), channel_id=1, source_target_pairs={{1,0},{2,1},{3,2},{4,3},{5,4},{6,5},{7,6},{0,7},{9,8},{10,9},{11,1... | collective-permute-start | bytes 776 | tf_op jit(solution)/shard_map/ppermute | solution.py:26
  4.2 13.6 %collective-permute-start = (bf16[32,4,1024]{2,1,0:T(4,128)(2,1)S(1)}, bf16[32,4,1024]{2,1,0:T(4,128)(2,1)S(1)}, u32[]{:S(2)}, u32[]{:S(2)}) collective-permute-start(bf16[32,4,1024]{2,1,0:T(4,128)(2,1)S(1)} %get-tuple-element.11), channel_id=1, source_target_pairs={{0,1},{1,2},{2,3},{3,4},{4,5},{5,6},{6,7},{7,0},{8,9},{9,10},{10,1... | collective-permute-start | bytes 786440 | tf_op jit(solution)/shard_map/ppermute | solution.py:25
  6.0 11.8 %collective-permute-start.1 = (bf16[32,4,1024]{2,1,0:T(4,128)(2,1)S(1)}, bf16[32,4,1024]{2,1,0:T(4,128)(2,1)S(1)}, u32[]{:S(2)}, u32[]{:S(2)}) collective-permute-start(bf16[32,4,1024]{2,1,0:T(4,128)(2,1)S(1)} %get-tuple-element.12), channel_id=1, source_target_pairs={{1,0},{2,1},{3,2},{4,3},{5,4},{6,5},{7,6},{0,7},{9,8},{10,9},{11,1... | collective-permute-start | bytes 786440 | tf_op jit(solution)/shard_map/ppermute | solution.py:26
  9.3 6.1 %collective-permute-start.6 = (bf16[4,40]{1,0:T(4,128)(2,1)S(1)}, bf16[4,40]{1,0:T(4,128)(2,1)S(1)}, u32[]{:S(2)}, u32[]{:S(2)}) collective-permute-start(bf16[4,40]{1,0:T(4,128)(2,1)S(1)} %get-tuple-element.13), channel_id=1, source_target_pairs={{0,8},{8,16},{16,24},{1,9},{9,17},{17,25},{2,10},{10,18},{18,26},{... | collective-permute-start | bytes 968 | tf_op jit(solution)/shard_map/ppermute | solution.py:25
  12.4 5.2 %collective-permute-start.7 = (bf16[4,40]{1,0:T(4,128)(2,1)S(1)}, bf16[4,40]{1,0:T(4,128)(2,1)S(1)}, u32[]{:S(2)}, u32[]{:S(2)}) collective-permute-start(bf16[4,40]{1,0:T(4,128)(2,1)S(1)} %get-tuple-element.14), channel_id=1, source_target_pairs={{8,0},{16,8},{24,16},{9,1},{17,9},{25,17},{10,2},{18,10},{26,18},{... | collective-permute-start | bytes 968 | tf_op jit(solution)/shard_map/ppermute | solution.py:26
  19.1 7.8 %collective-permute-start.2 = (bf16[4,40,1024]{2,1,0:T(8,128)(2,1)S(1)}, bf16[4,40,1024]{2,1,0:T(8,128)(2,1)S(1)}, u32[]{:S(2)}, u32[]{:S(2)}) collective-permute-start(bf16[4,40,1024]{2,1,0:T(8,128)(2,1)S(1)} %get-tuple-element.9), channel_id=1, source_target_pairs={{0,8},{8,16},{16,24},{1,9},{9,17},{17,25},{2,10},{10,18},{18,26},{... | collective-permute-start | bytes 983048 | tf_op jit(solution)/shard_map/ppermute | solution.py:25
  21.3 11.4 %collective-permute-start.3 = (bf16[4,40,1024]{2,1,0:T(8,128)(2,1)S(1)}, bf16[4,40,1024]{2,1,0:T(8,128)(2,1)S(1)}, u32[]{:S(2)}, u32[]{:S(2)}) collective-permute-start(bf16[4,40,1024]{2,1,0:T(8,128)(2,1)S(1)} %get-tuple-element.10), channel_id=1, source_target_pairs={{8,0},{16,8},{24,16},{9,1},{17,9},{25,17},{10,2},{18,10},{26,18},{... | collective-permute-start | bytes 983048 | tf_op jit(solution)/shard_map/ppermute | solution.py:26
